TPU v7x, 128 devices: a whole 4x4x4 slice. The times are simulated.
128 devices in a mesh: blk: 64 (over y, z_hi, x, core), grp: 2 (over z_lo).
Axes of the slice: x: 4, y: 4, z: 4 (z_hi: 2, z_lo: 2; z = z_hi * 2 + z_lo), core: 2. Of those that a mesh axis runs over, the one named last changes fastest.
Arguments:
- orbitals: float32 [64, 128, 128, 128], P(None, 'blk', 'grp'), may hold values from -6 to 6
- occupations: float32 [64], replicated, may hold values from 0.5 to 2
- band_block: int32 [64], replicated, may hold values from 0 to 63, as said below
- cycle: int32 [64], replicated, may hold values from 0 to 63, each once
Outputs:
- exchange_field: float32 [64, 128, 128, 128], P(None, 'blk', 'grp')
Inputs may be any that keep to these rules, and one draw needn't show every extreme that they name: `band_block`: each of the 64 blocks is named by exactly one band. Each block stands at exactly one cycle position.
All inputs are finite; a program needn't handle non-finite values.
Results may differ from a plain program's by a relative error of at most 0.0003.
Values sent between devices are 32-bit elements; how exact they have to be, the bound alone decides.
A program may use at most 128 MiB of HBM per device.

v0:
```python
import math

import jax
import jax.numpy as jnp
from jax import lax
from jax.sharding import PartitionSpec as P

screening = 0.05


def from_behind(block, axis, distance):
    devices = range(lax.axis_size(axis))
    route = [((i - distance) % len(devices), i) for i in devices]
    return lax.ppermute(block, axis, route)


def hartley(length):
    index = jnp.arange(length, dtype=jnp.int32)
    product = index[:, None] * index[None, :] % length
    angle = 2.0 * math.pi / length * product.astype(jnp.float32)
    return jnp.cos(angle) + jnp.sin(angle)


def kernel_table(size_x, size_y, size_z):

    def squared(length):
        index = jnp.arange(length, dtype=jnp.int32)
        folded = jnp.where(index <= length // 2, index, index - length).astype(jnp.float32)
        return (2.0 * math.pi / length * folded) ** 2

    total = (
        squared(size_x)[:, None, None]
        + squared(size_y)[None, :, None]
        + squared(size_z)[None, None, :]
    )
    safe_total = jnp.where(total > 0, total, 1.0)
    screened = (1.0 - jnp.exp(-safe_total / (4.0 * screening**2))) / safe_total
    return jnp.where(total > 0, screened, 1.0 / (4.0 * screening**2))


def potentials(density, tables):
    hart_x, hart_y, hart_z, kernel_half, volume = tables
    highest = lax.Precision.HIGHEST
    forward = jnp.einsum("pxyz,kx->pkyz", density, hart_x, precision=highest)
    forward = jnp.einsum("pkyz,lz->pkyl", forward, hart_z, precision=highest)
    turned = jnp.einsum(
        "pxyz,ky->pxkz",
        lax.all_to_all(forward, "grp", split_axis=1, concat_axis=2, tiled=True),
        hart_y,
        precision=highest,
    )
    turned = jnp.einsum("pxkz,yk->pxyz", turned * kernel_half[None], hart_y, precision=highest)
    returned = lax.all_to_all(turned, "grp", split_axis=2, concat_axis=1, tiled=True)
    returned = jnp.einsum("pkyz,xk->pxyz", returned, hart_x, precision=highest)
    returned = jnp.einsum("pxyl,zl->pxyz", returned, hart_z, precision=highest)
    return returned / volume


def pair_terms(first, first_weight, second, second_weight, tables):
    count_first = first.shape[0]
    count_second = second.shape[0]
    density = (first[:, None] * second[None, :]).reshape(
        (count_first * count_second,) + first.shape[1:]
    )
    field = potentials(density, tables).reshape((count_first, count_second) + first.shape[1:])
    to_first = jnp.sum(field * (second_weight[:, None, None, None] * second)[None], axis=1)
    to_second = jnp.sum(field * (first_weight[:, None, None, None] * first)[:, None], axis=0)
    return (to_first, to_second)


def local(orbitals, occupations, band_block, cycle):
    blocks = lax.axis_size("blk")
    groups = lax.axis_size("grp")
    position = lax.axis_index("blk")
    nbands, local_x, half_y, size_z = orbitals.shape
    band_dev = nbands // blocks
    size_x = local_x * blocks
    size_y = half_y * groups
    kernel_full = kernel_table(size_x, size_y, size_z)
    kernel_half = lax.dynamic_slice_in_dim(
        kernel_full, lax.axis_index("grp") * (size_x // groups), size_x // groups, 0
    )
    tables = (
        hartley(size_x),
        hartley(size_y),
        hartley(size_z),
        kernel_half,
        float(size_x * size_y * size_z),
    )
    order = jnp.argsort(band_block, stable=True)
    cycle_rows = order.reshape(blocks, band_dev)[cycle].reshape(-1)
    weights = occupations[cycle_rows].reshape(blocks, band_dev)
    picked = orbitals.reshape(nbands, -1)[cycle_rows]
    local_block = lax.all_to_all(picked, "blk", split_axis=0, concat_axis=1, tiled=True).reshape(
        band_dev, size_x, half_y, size_z
    )

    def weight_at(offset):
        return lax.dynamic_index_in_dim(weights, (position + offset) % blocks, 0, keepdims=False)

    own_weight = weight_at(0)
    visitor = local_block
    own_sum = jnp.zeros_like(local_block)
    returned_parts = []
    for offset in (1, 2):
        visitor = from_behind(visitor, "blk", 1)
        to_first, to_second = pair_terms(
            local_block, own_weight, visitor, weight_at(-offset), tables
        )
        own_sum = own_sum + to_first
        returned_parts.append(to_second)
    stacked = jnp.concatenate([own_sum] + returned_parts, axis=0)
    offsets = (0, -1, -2)
    count = len(offsets)
    received = lax.all_to_all(
        stacked.reshape(count * band_dev, -1), "blk", split_axis=1, concat_axis=0, tiled=True
    )
    received = received.reshape(blocks, count, band_dev, -1)
    placed = jnp.roll(received[:, 0], offsets[0], axis=0)
    for slot in range(1, count):
        placed = placed + jnp.roll(received[:, slot], offsets[slot], axis=0)
    flat = placed.reshape(nbands, -1)
    inverse = (
        jnp.zeros((nbands,), jnp.int32).at[cycle_rows].set(jnp.arange(nbands, dtype=jnp.int32))
    )
    return flat[inverse].reshape(orbitals.shape)


def solution(mesh):
    return jax.shard_map(
        local,
        mesh=mesh,
        in_specs=(P(None, "blk", "grp", None), P(), P(), P()),
        out_specs=P(None, "blk", "grp", None),
        check_vma=False,
    )
```

profile of v0, /device:TPU:15, one launch (start us, length us, event | category | flops | bytes accessed | tf_op | source)
XLA Modules:
  0.0 740.9 jit_solution(16803622640096036368)
XLA Ops:
  4.2 6.6 copy.83
  10.7 7.6 %gather_fusion.1 = f32[64,16384]{1,0:T(8,128)} fusion(f32[64,16384]{1,0:T(8,128)} %bitcast.158, s32[1024]{0:T(1024)S(1)} %pad_clamp_fusion.1), kind=kCustom, calls=%fused_computation.1 | custom fusion | bytes 8388864 | tf_op jit(solution)/shard_map/gather | solution.py:93
  18.4 6.5 copy.39
  24.9 61.1 %all_to_all.86 = f32[64,1,16384]{2,1,0:T(1,128)S(1)} all-to-all(f32[64,1,16384]{2,1,0:T(1,128)S(1)} %copy.39), channel_id=1, replica_groups=mesh['blk'=64,'grp'=2] {'blk'}, dimensions={0} | all-to-all | bytes 8388608 | tf_op jit(solution)/shard_map/all_to_all | solution.py:94
  91.8 45.4 %collective-permute-done = f32[1,128,64,128]{3,1,2,0:T(8,128)} collective-permute-done((f32[1,128,64,128]{3,1,2,0:T(8,128)S(1)}, f32[1,128,64,128]{3,1,2,0:T(8,128)}, u32[]{:S(2)}, u32[]{:S(2)}) %collective-permute-start) | collective-permute-done | bytes 4194336 | tf_op jit(solution)/shard_map/ppermute | solution.py:14
  137.2 6.2 collective-permute-start.1
  143.4 8.7 %fusion.13 = f32[128,64,128]{2,0,1:T(8,128)S(1)} fusion(f32[1,128,64,128]{3,1,2,0:T(8,128)} %collective-permute-done, f32[1,128,64,128]{3,2,1,0:T(8,128)S(1)} %bitcast.160), kind=kOutput, calls=%fused_computation.30 | convolution fusion | flops 1611907072 | bytes 12582912 | tf_op jit(solution)/shard_map/pxyz,kx->pkyz/dot_general | solution.py:44
  166.3 22.9 %collective-permute-done.1 = f32[1,128,64,128]{3,1,2,0:T(8,128)} collective-permute-done((f32[1,128,64,128]{3,1,2,0:T(8,128)}, f32[1,128,64,128]{3,1,2,0:T(8,128)}, u32[]{:S(2)}, u32[]{:S(2)}) %collective-permute-start.1) | collective-permute-done | bytes 4194336 | tf_op jit(solution)/shard_map/ppermute | solution.py:14
  189.2 9.2 %fusion.9 = f32[128,64,128]{2,0,1:T(8,128)S(1)} fusion(f32[1,128,64,128]{3,1,2,0:T(8,128)} %collective-permute-done.1, f32[1,128,64,128]{3,2,1,0:T(8,128)} %bitcast.161), kind=kOutput, calls=%fused_computation.25 | convolution fusion | flops 1611907072 | bytes 12582912 | tf_op jit(solution)/shard_map/pxyz,kx->pkyz/dot_general | solution.py:44
  209.2 5.6 all-to-all-start.3
  239.1 19.7 %all-to-all-done.3 = f32[1,128,64,128]{3,2,0,1:T(8,128)} async-done(((f32[1,128,64,128]{3,2,0,1:T(8,128)}), f32[1,128,64,128]{3,2,0,1:T(8,128)}, u32[]{:S(2)}, u32[]{:S(2)}) %all-to-all-start.3) | async-done | bytes 4194336 | tf_op jit(solution)/shard_map/all_to_all | solution.py:48
  258.8 5.6 all-to-all-start.2
  281.7 27.8 %all-to-all-done.2 = f32[1,64,128,128]{3,1,0,2:T(8,128)} async-done(((f32[1,64,128,128]{3,1,0,2:T(8,128)}), f32[1,64,128,128]{3,1,0,2:T(8,128)}, u32[]{:S(2)}, u32[]{:S(2)}) %all-to-all-start.2) | async-done | bytes 4194336 | tf_op jit(solution)/shard_map/all_to_all | solution.py:53
  321.9 6.3 fusion.17
  343.8 17.6 %all-to-all-done.4 = f32[1,64,128,128]{3,1,0,2:T(8,128)} async-done(((f32[1,64,128,128]{3,1,0,2:T(8,128)}), f32[1,64,128,128]{3,1,0,2:T(8,128)}, u32[]{:S(2)}, u32[]{:S(2)}) %all-to-all-start.4) | async-done | bytes 4194336 | tf_op jit(solution)/shard_map/all_to_all | solution.py:53
  366.6 6.3 fusion.15
  372.9 10.0 %fusion.8 = (f32[1,128,64,128]{3,1,2,0:T(8,128)S(1)}, f32[128,64,128]{2,0,1:T(8,128)}) fusion(f32[128,64,128]{2,0,1:T(8,128)S(1)} %copy-done.4, f32[1,128,64,128]{3,1,2,0:T(8,128)} %collective-permute-done.1, f32[1,128,64,128]{3,1,2,0:T(8,128)} %collective-permute-done, f32[]{:T(128)} %bitcast.35, f32[]{:T(128)} %bitcast.20, f32[128,64,128]{2,0,1:T(8,128)S(1)} %fusion.15), kind=kOutput, calls=%fused_computation.24 | convolution fusion | flops 1617149952 | bytes 25165832 | tf_op jit(solution)/shard_map/pxyl,zl->pxyz/dot_general | solution.py:55
  392.3 6.5 copy.58
  403.8 8.9 %bitcast_multiply_fusion.3 = (f32[1,64,16384]{2,1,0:T(8,128)S(1)}, f32[1,64,16384]{2,1,0:T(8,128)S(1)}) fusion(f32[1,64,16384]{2,1,0:T(8,128)} %div.30, f32[64,1,16384]{2,1,0:T(1,128)} %copy-done.2, f32[]{:T(128)} %bitcast.36, f32[1,64,16384]{2,1,0:T(8,128)} %div.31), kind=kLoop, calls=%fused_computation.22 | loop fusion | flops 3145728 | bytes 20971524 | tf_op jit(solution)/shard_map/mul | solution.py:67
  414.0 12.0 %copy.59 = f32[3,64,16384]{2,0,1:T(4,128)} copy(f32[3,64,16384]{2,1,0:T(8,128)S(1)} %pad_maximum_fusion) | data formatting | bytes 25165824 | tf_op jit(solution)/shard_map/concatenate | solution.py:112
  426.0 45.3 %all-to-all-start.5 = ((f32[3,64,16384]{2,0,1:T(4,128)}), f32[3,64,16384]{2,0,1:T(4,128)}, u32[]{:S(2)}, u32[]{:S(2)}) async-start(f32[3,64,16384]{2,0,1:T(4,128)} %copy.59), calls=%async_computation.5 | async-start | bytes 33554432 | tf_op jit(solution)/shard_map/all_to_all | solution.py:115
  472.6 226.5 %all-to-all-done.5 = f32[3,64,16384]{2,0,1:T(4,128)} async-done(((f32[3,64,16384]{2,0,1:T(4,128)}), f32[3,64,16384]{2,0,1:T(4,128)}, u32[]{:S(2)}, u32[]{:S(2)}) %all-to-all-start.5) | async-done | bytes 12582944 | tf_op jit(solution)/shard_map/all_to_all | solution.py:115
  699.0 17.6 %copy.82 = f32[3,64,16384]{2,1,0:T(8,128)} copy(f32[3,64,16384]{2,0,1:T(4,128)} %all-to-all-done.5) | data formatting | bytes 25165824 | tf_op jit(solution)/shard_map/all_to_all | solution.py:115
  728.1 7.6 %gather_fusion.3 = f32[64,16384]{1,0:T(8,128)} fusion(f32[64,16384]{1,0:T(8,128)} %fusion.1, s32[1024]{0:T(1024)S(1)} %pad_clamp_fusion), kind=kCustom, calls=%fused_computation.3 | custom fusion | bytes 8388864 | tf_op jit(solution)/shard_map/gather | solution.py:126
  (70 shorter events, 142.6 us)
Async XLA Ops:
  0.0 315.3 %copy-start = (f32[64]{0:T(128)S(1)}, f32[64]{0:T(128)}, u32[]{:S(2)}) copy-start(f32[64]{0:T(128)} %param.5) | copy-start | bytes 772
  86.0 57.4 %copy-start.2 = (f32[64,1,16384]{2,1,0:T(1,128)}, f32[64,1,16384]{2,1,0:T(1,128)S(1)}, u32[]{:S(2)}) copy-start(f32[64,1,16384]{2,1,0:T(1,128)S(1)} %all_to_all.86) | copy-start | bytes 12582916
  88.5 48.7 %collective-permute-start = (f32[1,128,64,128]{3,1,2,0:T(8,128)S(1)}, f32[1,128,64,128]{3,1,2,0:T(8,128)}, u32[]{:S(2)}, u32[]{:S(2)}) collective-permute-start(f32[1,128,64,128]{3,1,2,0:T(8,128)S(1)} %copy.41), channel_id=1, source_target_pairs={{126,0},{0,2},{2,4},{4,6},{6,8},{8,10},{10,12},{12,14},{14,16},{16... | collective-permute-start | bytes 12582920 | tf_op jit(solution)/shard_map/ppermute | solution.py:14
  137.2 52.0 %collective-permute-start.1 = (f32[1,128,64,128]{3,1,2,0:T(8,128)}, f32[1,128,64,128]{3,1,2,0:T(8,128)}, u32[]{:S(2)}, u32[]{:S(2)}) collective-permute-start(f32[1,128,64,128]{3,1,2,0:T(8,128)} %collective-permute-done), channel_id=1, source_target_pairs={{126,0},{0,2},{2,4},{4,6},{6,8},{8,10},{10,12},{12,14},{14,16},{16... | collective-permute-start | bytes 12582920 | tf_op jit(solution)/shard_map/ppermute | solution.py:14
  160.6 48.6 %all-to-all-start.1 = ((f32[1,128,64,128]{3,2,0,1:T(8,128)}), f32[1,128,64,128]{3,2,0,1:T(8,128)}, u32[]{:S(2)}, u32[]{:S(2)}) async-start(f32[1,128,64,128]{3,2,0,1:T(8,128)} %copy.42), calls=%async_computation.1 | async-start | bytes 8388608 | tf_op jit(solution)/shard_map/all_to_all | solution.py:48
  209.2 49.7 %all-to-all-start.3 = ((f32[1,128,64,128]{3,2,0,1:T(8,128)}), f32[1,128,64,128]{3,2,0,1:T(8,128)}, u32[]{:S(2)}, u32[]{:S(2)}) async-start(f32[1,128,64,128]{3,2,0,1:T(8,128)} %copy.49), calls=%async_computation.3 | async-start | bytes 8388608 | tf_op jit(solution)/shard_map/all_to_all | solution.py:48
  217.1 11.9 %copy-start.6 = (f32[128,128,128]{2,1,0:T(8,128)}, f32[128,128,128]{2,1,0:T(8,128)S(1)}, u32[]{:S(2)}) copy-start(f32[128,128,128]{2,1,0:T(8,128)S(1)} %add_select_fusion) | copy-start | bytes 25165828
  258.8 50.7 %all-to-all-start.2 = ((f32[1,64,128,128]{3,1,0,2:T(8,128)}), f32[1,64,128,128]{3,1,0,2:T(8,128)}, u32[]{:S(2)}, u32[]{:S(2)}) async-start(f32[1,64,128,128]{3,1,0,2:T(8,128)} %copy.44), calls=%async_computation.2 | async-start | bytes 8388608 | tf_op jit(solution)/shard_map/all_to_all | solution.py:53
  264.5 7.0 slice-start
  267.1 4.3 slice-start.1
  309.6 51.8 %all-to-all-start.4 = ((f32[1,64,128,128]{3,1,0,2:T(8,128)}), f32[1,64,128,128]{3,1,0,2:T(8,128)}, u32[]{:S(2)}, u32[]{:S(2)}) async-start(f32[1,64,128,128]{3,1,0,2:T(8,128)} %copy.51), calls=%async_computation.4 | async-start | bytes 8388608 | tf_op jit(solution)/shard_map/all_to_all | solution.py:53
  332.4 2.0 copy-start.3
  366.6 6.3 copy-start.4
  403.8 8.9 %copy-start.5 = (f32[1,64,16384]{2,1,0:T(8,128)S(1)}, f32[1,64,16384]{2,1,0:T(8,128)}, u32[]{:S(2)}) copy-start(f32[1,64,16384]{2,1,0:T(8,128)} %concatenate.29) | copy-start | bytes 12582916
  426.0 273.0 %all-to-all-start.5 = ((f32[3,64,16384]{2,0,1:T(4,128)}), f32[3,64,16384]{2,0,1:T(4,128)}, u32[]{:S(2)}, u32[]{:S(2)}) async-start(f32[3,64,16384]{2,0,1:T(4,128)} %copy.59), calls=%async_computation.5 | async-start | bytes 33554432 | tf_op jit(solution)/shard_map/all_to_all | solution.py:115
  735.8 5.0 copy-start.1
where the time goes:
time: 750 us; the launch traced here: 741 us
  waiting for transfers between devices  362 us (48%)
  local copies, waits for them, and re-layouts  142 us (19%)
  starting transfers between devices  77.3 us (10%)
  matrix products  71.8 us (10%)
  blocking collectives  61.1 us (8%)
  other arithmetic  25.4 us (3%)
    all_to_all x1, waiting for transfers between devices, local(): lax.all_to_all(stacked.reshape(count * band_dev, -1), 'blk', split_axis=1...  226 us
    ppermute x2, waiting for transfers between devices, from_behind(): return lax.ppermute(block, axis, route)  68.3 us
    all_to_all x1, blocking collectives, local(): lax.all_to_all(picked, 'blk', split_axis=0, concat_axis=1, tiled=True)  61.1 us
    all_to_all x2, waiting for transfers between devices, potentials(): lax.all_to_all(turned, 'grp', split_axis=2, concat_axis=1, tiled=True)  45.5 us
    all_to_all x1, starting transfers between devices, local(): lax.all_to_all(stacked.reshape(count * band_dev, -1), 'blk', split_axis=1...  45.3 us
    all_to_all x2, waiting for transfers between devices, potentials(): lax.all_to_all(forward, 'grp', split_axis=1, concat_axis=2, tiled=True)  22.2 us
    div x4, local copies, waits for them, and re-layouts, potentials(): return returned / volume  20.9 us
    dot_general x2, matrix products, potentials(): forward = jnp.einsum('pxyz,kx->pkyz', density, hart_x, precision=highest)  17.8 us
  transfers between devices with their start and end apart: 7, of which 7 were waited for; matrix products, arithmetic and copies ran while one was open for 14% of the time, Pallas kernels for 0%

commit v1 on v0

v1 whole, which is shorter than its diff:
```python
import functools
import math

import jax
import jax.numpy as jnp
import ml_dtypes
import numpy as np
from jax import lax
from jax.experimental import pallas as pl
from jax.experimental.pallas import tpu as pltpu
from jax.sharding import PartitionSpec as P

screening = 0.05
MESH = pl.DeviceIdType.MESH
MIB = 2**20


def hartley_split(length):
    index = np.arange(length)
    angle = 2.0 * math.pi / length * (index[:, None] * index[None, :] % length)
    exact = (np.cos(angle) + np.sin(angle)).astype(np.float64)
    high = exact.astype(ml_dtypes.bfloat16)
    low = (exact - high.astype(np.float64)).astype(ml_dtypes.bfloat16)
    return np.block([[high, low], [high, np.zeros_like(high)]])


def split(value, axis):
    high = value.astype(jnp.bfloat16)
    low = (value - high.astype(jnp.float32)).astype(jnp.bfloat16)
    return jnp.concatenate([high, low], axis=axis)


def times_right(value, table):
    length = table.shape[0] // 2
    both = jnp.dot(split(value, 1), table, preferred_element_type=jnp.float32)
    return both[:, :length] + both[:, length:]


def times_left(table, value):
    length = table.shape[0] // 2
    both = jnp.dot(table, split(value, 0), preferred_element_type=jnp.float32)
    return both[:length] + both[length:]


def squared(index, length):
    folded = jnp.where(index <= length // 2, index, index - length).astype(jnp.float32)
    return (2.0 * math.pi / length * folded) ** 2


def exchange_kernel(
    sizes,
    rows_ref,
    weight_ref,
    phi_ref,
    right_z_ref,
    left_y_ref,
    left_x_ref,
    field_ref,
    outgoing,
    grid,
    turned,
    kernel_table,
    arrived,
    out_sem,
    in_sem,
    back_out_sem,
    back_in_sem,
):
    blocks, size_x, size_y, size_z, local_x = sizes
    half_y = size_y // 2
    plane_rows = local_x * half_y
    blk = lax.axis_index("blk")
    grp = lax.axis_index("grp")
    other = 1 - grp
    me = blk * 2 + grp

    def hop(step):
        return (step * (step + 1) // 2) % blocks

    barrier = pltpu.get_barrier_semaphore()
    pl.semaphore_signal(barrier, inc=1, device_id=(blk, other), device_id_type=MESH)

    @pl.loop(1, blocks)
    def _(step):
        target = (blk + hop(step)) % blocks
        for side in range(2):
            pl.semaphore_signal(barrier, inc=1, device_id=(target, side), device_id_type=MESH)

    pl.semaphore_wait(barrier, 2 * blocks - 1)

    def density(position, offset):
        first = phi_ref[rows_ref[position]]
        second = phi_ref[rows_ref[(position + blocks - offset) % blocks]]
        return times_right(first * second, right_z_ref[...])

    def here(ref):
        return ref.at[pl.ds(blk * local_x, local_x), pl.ds(grp * half_y, half_y)]

    def send(target, side, slot):
        outgoing[slot] = density(target, side + 1).reshape(local_x, half_y, size_z)
        pltpu.make_async_remote_copy(
            src_ref=outgoing.at[slot],
            dst_ref=here(grid),
            send_sem=out_sem,
            recv_sem=in_sem.at[blk],
            device_id=(target, side),
            device_id_type=MESH,
        ).start()

    send(blk, other, 1)

    @pl.loop(1, blocks)
    def _(step):
        target = (blk + hop(step)) % blocks
        for side in range(2):
            send(target, side, 2 * step + side)

    own = density(blk, grp + 1).reshape(local_x, half_y, size_z)
    grid[pl.ds(blk * local_x, local_x), pl.ds(grp * half_y, half_y)] = own
    field_ref[...] = jnp.zeros_like(field_ref)

    across = squared(lax.broadcasted_iota(jnp.int32, (size_x, size_z), 0), size_x) + squared(
        lax.broadcasted_iota(jnp.int32, (size_x, size_z), 1), size_z
    )

    @pl.loop(0, size_y // 2 + 1)
    def _(index):
        total = across + squared(jnp.full((size_x, size_z), index, jnp.int32), size_y)
        safe_total = jnp.where(total > 0, total, 1.0)
        screened = (1.0 - jnp.exp(-safe_total / (4.0 * screening**2))) / safe_total
        value = jnp.where(total > 0, screened, 1.0 / (4.0 * screening**2))
        kernel_table[index] = value * (1.0 / (size_x * size_y * size_z))

    def turn_planes(source):
        planes = [grid[source * local_x + j] for j in range(local_x)]
        result = times_left(left_y_ref[...], jnp.concatenate(planes, axis=1))
        for j in range(local_x):
            turned[pl.ds(source * local_x + j, size_y, stride=size_x), :] = result[
                :, j * size_z : (j + 1) * size_z
            ]

    half_plane = here(grid)
    pltpu.make_async_copy(half_plane, half_plane, in_sem.at[blk]).wait()
    turn_planes(blk)

    @pl.loop(1, blocks)
    def _(step):
        source = (blk + blocks - hop(step)) % blocks
        landed = grid.at[pl.ds(source * local_x, local_x)]
        pltpu.make_async_copy(landed, landed, in_sem.at[source]).wait()
        turn_planes(source)

    group = 8

    @pl.loop(0, size_y // group)
    def _(part):
        lines = [part * group + j for j in range(group)]
        value = jnp.concatenate([turned[pl.ds(k * size_x, size_x), :] for k in lines], axis=1)
        value = times_left(left_x_ref[...], value)
        factor = [kernel_table[jnp.minimum(k, size_y - k)] for k in lines]
        value = times_left(left_x_ref[...], value * jnp.concatenate(factor, axis=1))
        for j, k in enumerate(lines):
            turned[pl.ds(k * size_x, size_x), :] = value[:, j * size_z : (j + 1) * size_z]

    def turn_back(target):
        lines = [
            turned[pl.ds(target * local_x + j, size_y, stride=size_x), :] for j in range(local_x)
        ]
        result = times_left(left_y_ref[...], jnp.concatenate(lines, axis=1))
        for j in range(local_x):
            grid[target * local_x + j] = result[:, j * size_z : (j + 1) * size_z]

    def send_back(target, side):
        pltpu.make_async_remote_copy(
            src_ref=grid.at[pl.ds(target * local_x, local_x), pl.ds(side * half_y, half_y)],
            dst_ref=arrived.at[me],
            send_sem=back_out_sem,
            recv_sem=back_in_sem.at[blk],
            device_id=(target, side),
            device_id_type=MESH,
        ).start()

    turn_back(blk)
    send_back(blk, other)

    @pl.loop(1, blocks)
    def _(step):
        target = (blk + hop(step)) % blocks
        turn_back(target)
        for side in range(2):
            send_back(target, side)

    arrived[me] = grid[pl.ds(blk * local_x, local_x), pl.ds(grp * half_y, half_y)]

    def collect(position):
        def weighted(at):
            return weight_ref[at] * phi_ref[rows_ref[at]]

        own = weighted(position)
        total = jnp.zeros((plane_rows, size_z), jnp.float32)
        for offset in (1, 2):
            behind = (position + blocks - offset) % blocks
            value = arrived[position * 2 + offset - 1].reshape(plane_rows, size_z)
            value = times_right(value, right_z_ref[...])
            total = total + value * weighted(behind)
            field_ref[behind] += value * own
        field_ref[position] += total

    pltpu.make_async_copy(arrived.at[me], arrived.at[me], back_in_sem.at[blk]).wait()
    collect(blk)

    @pl.loop(1, blocks)
    def _(step):
        source = (blk + blocks - hop(step)) % blocks
        landed = arrived.at[pl.ds(source * 2, 2)]
        pltpu.make_async_copy(landed, landed, back_in_sem.at[source]).wait()
        collect(source)

    sent = outgoing.at[pl.ds(1, 2 * blocks - 1)]
    pltpu.make_async_copy(sent, sent, out_sem).wait()
    pltpu.make_async_copy(sent, sent, back_out_sem).wait()


def place_kernel(nbands, rows_ref, field_ref, out_ref, sem):
    copies = [
        pltpu.make_async_copy(field_ref.at[p], out_ref.at[rows_ref[p]], sem.at[p])
        for p in range(nbands)
    ]
    for copy in copies:
        copy.start()
    for copy in copies:
        copy.wait()


def local(orbitals, occupations, band_block, cycle):
    blocks = lax.axis_size("blk")
    nbands, local_x, half_y, size_z = orbitals.shape
    size_x = local_x * blocks
    size_y = half_y * 2
    plane_rows = local_x * half_y
    f32 = jnp.float32

    here = cycle[:, None] == band_block[None, :]
    rows = jnp.sum(jnp.where(here, jnp.arange(nbands, dtype=jnp.int32)[None], 0), axis=1)
    weights = jnp.sum(jnp.where(here, occupations[None], 0.0), axis=1)

    vmem = pl.BlockSpec(memory_space=pltpu.VMEM)
    smem = pl.BlockSpec(memory_space=pltpu.SMEM)
    field = pl.pallas_call(
        functools.partial(exchange_kernel, (blocks, size_x, size_y, size_z, local_x)),
        out_shape=jax.ShapeDtypeStruct((nbands, plane_rows, size_z), f32),
        in_specs=[smem, smem, vmem, vmem, vmem, vmem],
        out_specs=vmem,
        scratch_shapes=[
            pltpu.VMEM((2 * blocks, local_x, half_y, size_z), f32),
            pltpu.VMEM((size_x, size_y, size_z), f32),
            pltpu.VMEM((size_y * size_x, size_z), f32),
            pltpu.VMEM((size_y // 2 + 1, size_x, size_z), f32),
            pltpu.VMEM((2 * blocks, local_x, half_y, size_z), f32),
            pltpu.SemaphoreType.DMA,
            pltpu.SemaphoreType.DMA((blocks,)),
            pltpu.SemaphoreType.DMA,
            pltpu.SemaphoreType.DMA((blocks,)),
        ],
        compiler_params=pltpu.CompilerParams(
            collective_id=0, has_side_effects=True, vmem_limit_bytes=60 * MIB
        ),
    )(
        rows,
        weights,
        orbitals.reshape(nbands, plane_rows, size_z),
        jnp.asarray(hartley_split(size_z)),
        jnp.asarray(hartley_split(size_y).T),
        jnp.asarray(hartley_split(size_x).T),
    )
    placed = pl.pallas_call(
        functools.partial(place_kernel, nbands),
        out_shape=jax.ShapeDtypeStruct((nbands, plane_rows, size_z), f32),
        in_specs=[smem, pl.BlockSpec(memory_space=pl.ANY)],
        out_specs=pl.BlockSpec(memory_space=pl.ANY),
        scratch_shapes=[pltpu.SemaphoreType.DMA((nbands,))],
    )(rows, field)
    return placed.reshape(orbitals.shape)


def solution(mesh):
    return jax.shard_map(
        local,
        mesh=mesh,
        in_specs=(P(None, "blk", "grp", None), P(), P(), P()),
        out_specs=P(None, "blk", "grp", None),
        check_vma=False,
    )
```

time: 750 us -> 400 us (0.53)
  the two profiles are of different devices: /device:TPU:15 before, /device:TPU:51 now
where the time goes in v1:
time: 400 us
  Pallas kernels  398 us (100%)
    pallas_call x1, Pallas kernels, local(): pl.pallas_call(functools.partial(exchange_kernel, (blocks, size_x, size_y...  268 us
    pallas_call x1, Pallas kernels, local(): pl.pallas_call(functools.partial(place_kernel, nbands), out_shape=jax.Sha...  129 us

profile of v1, /device:TPU:51, one launch (start us, length us, event | category | flops | bytes accessed | tf_op | source)
XLA Modules:
  0.0 400.4 jit_solution(7366487624048159906)
XLA Ops:
  0.0 1.4 fusion.rows_ref
  1.4 1.4 fusion.1.weight_ref
  2.8 268.2 %shard_map.73.field_ref = f32[64,128,128]{2,1,0:T(8,128)} custom-call(s32[64]{0:T(128)} %fusion.rows_ref, f32[64]{0:T(128)} %fusion.1.weight_ref, f32[64,128,128]{2,1,0:T(8,128)} %bitcast.2, bf16[256,256]{1,0:T(8,128)(2,1)} %constant.8.clone.right_z_ref, bf16[256,256]{1,0:T(8,128)(2,1)} %constant.9.clone.left_y_ref.left_x_ref, ...), custom_call_target="tpu_custom_call" | custom-call | tf_op jit(solution)/shard_map/pallas_call | solution.py:249
  270.9 129.4 %shard_map.74 = f32[64,128,128]{2,1,0:T(8,128)} custom-call(s32[64]{0:T(128)} %fusion.rows_ref, f32[64,128,128]{2,1,0:T(8,128)} %shard_map.73.field_ref), custom_call_target="tpu_custom_call" | custom-call | tf_op jit(solution)/shard_map/pallas_call | solution.py:276

commit v2 on v1

v2 whole, which is shorter than its diff:
```python
import functools
import itertools
import math
import random

import jax
import jax.numpy as jnp
import ml_dtypes
import numpy as np
from jax import lax
from jax.experimental import pallas as pl
from jax.experimental.pallas import tpu as pltpu
from jax.sharding import PartitionSpec as P

screening = 0.05
MESH = pl.DeviceIdType.MESH
MIB = 2**20
f32 = jnp.float32


def hartley(length):
    index = np.arange(length)
    angle = 2.0 * math.pi / length * (index[:, None] * index[None, :] % length)
    return np.cos(angle) + np.sin(angle)


def pieces(table, axis):
    high = table.astype(ml_dtypes.bfloat16)
    low = (table - high.astype(np.float64)).astype(ml_dtypes.bfloat16)
    return jnp.asarray(np.concatenate([high, high, low], axis=axis))


def split(value, axis):
    high = value.astype(jnp.bfloat16)
    low = (value - high.astype(f32)).astype(jnp.bfloat16)
    return jnp.concatenate([high, low, high], axis=axis)


def times_right(value, table):
    return jnp.dot(split(value, 1), table, preferred_element_type=f32)


def times_left(table, value):
    return jnp.dot(table, split(value, 0), preferred_element_type=f32)


def planes_table(size_z):
    half = size_z // 2
    table = hartley(size_z)
    full = np.zeros((2, size_z, 2, 2, half))
    for plane in range(2):
        for part in range(2):
            full[plane, :, part, plane, :] = table[:, part * half : (part + 1) * half]
    return full.reshape(2 * size_z, 2 * size_z)


def torus_of(blocks):
    return (4, 4, 4) if blocks == 64 else (blocks // 2, 1, 2)


def message_order(blocks):
    torus = torus_of(blocks)
    everywhere = itertools.product(*(range(size) for size in torus))
    triples, seen = [], {(0, 0, 0)}
    for offset in everywhere:
        if offset not in seen:
            turns = [offset]
            if torus[0] == torus[1] == torus[2]:
                turns = list(dict.fromkeys(offset[k:] + offset[:k] for k in range(3)))
            seen.update(turns)
            triples.append(turns)
    random.Random(1).shuffle(triples)
    triples.sort(key=lambda turns: sum(min(d, n - d) for d, n in zip(turns[0], torus)))
    mixed = []
    while triples:
        mixed.append(triples.pop(0))
        if triples:
            mixed.append(triples.pop())
    order = [(0, 0, 0, 1)]
    order += [d + (core,) for turns in mixed for core in (0, 1) for d in turns]
    return order + [(0, 0, 0, 0)]


def source_order(blocks, parity):
    torus = torus_of(blocks)
    due = {}
    for time, (dx, dy, dz, core) in enumerate(message_order(blocks)):
        sign = -1 if core else 1
        offset = [sign * d % n for d, n in zip((dx, dy, dz), torus)]
        block = (offset[0], offset[1], (parity - offset[2]) % torus[2] // 2, core)
        due[block] = (time, tuple(offset) + (core,))
    own = (0, 0, parity // 2, 0)
    rest = sorted(due[block] for block in due if block != own)
    return [(0, 0, 0, 0)] + [offset for time, offset in rest]


def packed(order):
    codes = [dx + 4 * dy + 16 * dz + 64 * core for dx, dy, dz, core in order]
    return [sum(c * 128**j for j, c in enumerate(codes[i : i + 4])) for i in range(0, len(codes), 4)]


def word_at(words, index):
    word = jnp.int32(words[0])
    for k in range(1, len(words)):
        word = jnp.where(index == k, jnp.int32(words[k]), word)
    return word


def offsets_in(word):
    for j in range(4):
        code = word // 128**j % 128
        yield code % 4, code // 4 % 4, code // 16 % 4, code // 64


def squared(index, length):
    folded = jnp.where(index <= length // 2, index, index - length).astype(f32)
    return (2.0 * math.pi / length * folded) ** 2


def exchange_kernel(
    sizes,
    rows_ref,
    weight_ref,
    phi_ref,
    forward_z_ref,
    inverse_z_ref,
    left_y_ref,
    forward_x_ref,
    inverse_x_ref,
    field_ref,
    outgoing,
    grid,
    turned,
    kernel_table,
    arrived,
    out_sem,
    in_sem,
    back_out_sem,
    back_in_sem,
):
    blocks, size_x, size_y, size_z = sizes
    half_y = size_y // 2
    half_z = size_z // 2
    blk = lax.axis_index("blk")
    grp = lax.axis_index("grp")
    me = blk * 2 + grp
    own_rows = pl.ds(grp * half_y, half_y)

    span_x, span_y, span_z = torus_of(blocks)
    core = blk % 2
    at_x = blk // 2 % span_x
    at_y = blk // (span_x * span_z)
    at_z = blk // (2 * span_x) % (span_z // 2) * 2 + grp
    sign = 1 - 2 * core
    messages = packed(message_order(blocks))
    sources = [packed(source_order(blocks, parity)) for parity in range(2)]

    def device(offset, direction):
        x, y, z, other_core = offset
        x = (at_x + direction * x + span_x) % span_x
        y = (at_y + direction * y + span_y) % span_y
        z = (at_z + direction * z + span_z) % span_z
        block = (y * (span_z // 2) + z // 2) * span_x + x
        return block * 2 + (core + other_core) % 2, z % 2

    def targets(index):
        return [device(offset, sign) for offset in offsets_in(word_at(messages, index))]

    def source_blocks(index):
        pairs = [word_at(sources[parity], index) for parity in range(2)]
        word = jnp.where((core + grp) % 2 == 0, pairs[0], pairs[1])
        return [device(offset, -sign)[0] for offset in offsets_in(word)]

    count = 2 * blocks

    def every_other(act):
        @pl.loop(0, count // 4 - 1)
        def _(index):
            for j, target in enumerate(targets(index)):
                act(index * 4 + j, target)

        for j, target in enumerate(targets(count // 4 - 1)[:3]):
            act(count - 4 + j, target)

    barrier = pltpu.get_barrier_semaphore()

    def greet(slot, target):
        pl.semaphore_signal(barrier, inc=1, device_id=target, device_id_type=MESH)

    every_other(greet)
    pl.semaphore_wait(barrier, count - 1)

    def density(position, offset):
        first = phi_ref[rows_ref[position]]
        second = phi_ref[rows_ref[(position + blocks - offset) % blocks]]
        value = first * second
        return jnp.concatenate([value[:half_y], value[half_y:]], axis=1)

    def send(part, slot, target):
        pltpu.make_async_remote_copy(
            src_ref=outgoing.at[part, slot],
            dst_ref=grid.at[part, blk, own_rows],
            send_sem=out_sem,
            recv_sem=in_sem.at[part, blk],
            device_id=target,
            device_id_type=MESH,
        ).start()

    def prepare(index, sent):
        at = targets(index)
        value = jnp.concatenate([density(b, side + 1) for b, side in at], axis=0)
        value = times_right(value, forward_z_ref[...])
        for j in range(4):
            for part in range(2):
                outgoing[part, index * 4 + j] = value[
                    j * half_y : (j + 1) * half_y, part * size_z : (part + 1) * size_z
                ]
        for j in range(sent):
            send(0, index * 4 + j, at[j])

    @pl.loop(0, count // 4 - 1)
    def _(index):
        prepare(index, 4)

    prepare(count // 4 - 1, 3)
    every_other(functools.partial(send, 1))
    for part in range(2):
        grid[part, blk, own_rows] = outgoing[part, count - 1]
    field_ref[...] = jnp.zeros_like(field_ref)

    lane = lax.broadcasted_iota(jnp.int32, (size_x, size_z), 1)
    first_half = lane < half_z
    lane_half = jnp.where(first_half, 0, 1)

    def fill_table(part):
        square_x = squared(lax.broadcasted_iota(jnp.int32, (size_x, size_z), 0), size_x)
        square_z = squared(lane - half_z * lane_half + part * half_z, size_z)

        @pl.loop(0, half_y)
        def _(pair):
            total = square_x + squared(2 * pair + lane_half, size_y) + square_z
            safe_total = jnp.where(total > 0, total, 1.0)
            screened = (1.0 - jnp.exp(-safe_total / (4.0 * screening**2))) / safe_total
            value = jnp.where(total > 0, screened, 1.0 / (4.0 * screening**2))
            kernel_table[part, pair] = value * (1.0 / (size_x * size_y * size_z))

    def await_copy(ref, sem):
        pltpu.make_async_copy(ref, ref, sem).wait()

    def turn(part, index, with_own):
        at = source_blocks(index)
        for j, source in enumerate(at):
            if with_own and j == 0:
                await_copy(grid.at[part, blk, own_rows], in_sem.at[part, blk])
            else:
                await_copy(grid.at[part, source], in_sem.at[part, source])
        value = jnp.concatenate([grid[part, source] for source in at], axis=1)
        value = times_left(left_y_ref[...], value)
        for j, source in enumerate(at):
            turned[part, pl.ds(source, size_y, stride=blocks), :] = value[:, j * size_z : (j + 1) * size_z]

    def middle(part):
        group = 4
        mask = first_half[:blocks]

        @pl.loop(0, half_y // group)
        def _(index):
            pairs = [index * group + j for j in range(group)]
            lines = [2 * i + j for i in pairs for j in range(2)]
            value = [turned[part, pl.ds(k * blocks, blocks), :] for k in lines]
            both = times_left(forward_x_ref[...], jnp.concatenate(value, axis=1))
            value = []
            for j in range(group):
                a = both[:, 2 * j * size_z : (2 * j + 1) * size_z]
                b = both[:, (2 * j + 1) * size_z : (2 * j + 2) * size_z]
                stay = jnp.where(first_half, a[:size_x], b[size_x:])
                move = jnp.where(first_half, b[:size_x], a[size_x:])
                value.append((stay + pltpu.roll(move, half_z, 1)) * kernel_table[part, pairs[j]])
            both = times_left(inverse_x_ref[...], jnp.concatenate(value, axis=1))
            for j, i in enumerate(pairs):
                even = both[:blocks, j * size_z : (j + 1) * size_z]
                odd = both[blocks:, j * size_z : (j + 1) * size_z]
                moved = pltpu.roll(jnp.where(mask, odd, even), half_z, 1)
                turned[part, pl.ds(2 * i * blocks, blocks), :] = jnp.where(mask, even, moved)
                turned[part, pl.ds((2 * i + 1) * blocks, blocks), :] = jnp.where(mask, moved, odd)

    def turn_back(part, slot, target):
        block, side = target
        rows = pl.ds(pl.multiple_of(side * half_y, half_y), half_y)
        lines = turned[part, pl.ds(block, size_y, stride=blocks), :]
        grid[part, block, rows] = times_left(left_y_ref[rows, :], lines)

    def send_back(part, slot, target):
        block, side = target
        pltpu.make_async_remote_copy(
            src_ref=grid.at[part, block, pl.ds(side * half_y, half_y)],
            dst_ref=arrived.at[part, me],
            send_sem=back_out_sem,
            recv_sem=back_in_sem.at[part, blk],
            device_id=target,
            device_id_type=MESH,
        ).start()

    def give_back(part, index, sent):
        at = targets(index)
        for target in at:
            turn_back(part, None, target)
        for target in at[:sent]:
            send_back(part, None, target)

    for part in range(2):
        fill_table(part)
        turn(part, 0, True)

        @pl.loop(1, blocks // 4)
        def _(index):
            turn(part, index, False)

    for part in range(2):
        middle(part)

        @pl.loop(0, count // 4 - 1)
        def _(index):
            give_back(part, index, 4)

        give_back(part, count // 4 - 1, 3)
        arrived[part, me] = grid[part, blk, own_rows]

    def collect(index, with_own):
        at = source_blocks(index)
        for part in range(2):
            for j, source in enumerate(at):
                if with_own and j == 0:
                    await_copy(arrived.at[part, me], back_in_sem.at[part, blk])
                else:
                    landed = arrived.at[part, pl.ds(source * 2, 2)]
                    await_copy(landed, back_in_sem.at[part, source])
        slots = [source * 2 + side for source in at for side in range(2)]
        value = [jnp.concatenate([arrived[0, k], arrived[1, k]], axis=1) for k in slots]
        value = times_right(jnp.concatenate(value, axis=0), inverse_z_ref[...])
        for j, position in enumerate(at):
            own = weight_ref[position] * phi_ref[rows_ref[position]]
            total = jnp.zeros((size_y, size_z), f32)
            for side in range(2):
                behind = (position + blocks - side - 1) % blocks
                term = value[(2 * j + side) * half_y : (2 * j + side + 1) * half_y]
                term = jnp.concatenate([term[:, :size_z], term[:, size_z:]], axis=0)
                total = total + term * (weight_ref[behind] * phi_ref[rows_ref[behind]])
                field_ref[behind] += term * own
            field_ref[position] += total

    collect(0, True)

    @pl.loop(1, blocks // 4)
    def _(index):
        collect(index, False)

    for part in range(2):
        sent = outgoing.at[part, pl.ds(0, count - 1)]
        await_copy(sent, out_sem)
        await_copy(sent, back_out_sem)


def place_kernel(nbands, rows_ref, field_ref, out_ref, sem):
    copies = [
        pltpu.make_async_copy(field_ref.at[p], out_ref.at[rows_ref[p]], sem.at[p])
        for p in range(nbands)
    ]
    for copy in copies:
        copy.start()
    for copy in copies:
        copy.wait()


def local(orbitals, occupations, band_block, cycle):
    blocks = lax.axis_size("blk")
    nbands, local_x, half_y, size_z = orbitals.shape
    size_x = local_x * blocks
    size_y = half_y * 2
    plane_rows = local_x * half_y

    here = cycle[:, None] == band_block[None, :]
    rows = jnp.sum(jnp.where(here, jnp.arange(nbands, dtype=jnp.int32)[None], 0), axis=1)
    weights = jnp.sum(jnp.where(here, occupations[None], 0.0), axis=1)

    by_parity = hartley(size_x).reshape(size_x, blocks, 2)
    even_odd = by_parity.transpose(2, 0, 1).reshape(2 * size_x, blocks)
    odd_last = by_parity.transpose(2, 1, 0).reshape(size_x, size_x)
    tables = (
        pieces(planes_table(size_z), 0),
        pieces(planes_table(size_z).T, 0),
        pieces(hartley(size_y), 1),
        pieces(even_odd, 1),
        pieces(odd_last, 1),
    )

    vmem = pl.BlockSpec(memory_space=pltpu.VMEM)
    smem = pl.BlockSpec(memory_space=pltpu.SMEM)
    field = pl.pallas_call(
        functools.partial(exchange_kernel, (blocks, size_x, size_y, size_z)),
        out_shape=jax.ShapeDtypeStruct((nbands, plane_rows, size_z), f32),
        in_specs=[smem, smem] + [vmem] * (1 + len(tables)),
        out_specs=vmem,
        scratch_shapes=[
            pltpu.VMEM((2, 2 * blocks, half_y, size_z), f32),
            pltpu.VMEM((2, blocks, size_y, size_z), f32),
            pltpu.VMEM((2, size_y * blocks, size_z), f32),
            pltpu.VMEM((2, half_y, size_x, size_z), f32),
            pltpu.VMEM((2, 2 * blocks, half_y, size_z), f32),
            pltpu.SemaphoreType.DMA,
            pltpu.SemaphoreType.DMA((2, blocks)),
            pltpu.SemaphoreType.DMA,
            pltpu.SemaphoreType.DMA((2, blocks)),
        ],
        compiler_params=pltpu.CompilerParams(
            collective_id=0, has_side_effects=True, vmem_limit_bytes=60 * MIB
        ),
    )(rows, weights, orbitals.reshape(nbands, plane_rows, size_z), *tables)
    placed = pl.pallas_call(
        functools.partial(place_kernel, nbands),
        out_shape=jax.ShapeDtypeStruct((nbands, plane_rows, size_z), f32),
        in_specs=[smem, vmem],
        out_specs=pl.BlockSpec(memory_space=pl.ANY),
        scratch_shapes=[pltpu.SemaphoreType.DMA((nbands,))],
    )(rows, field)
    return placed.reshape(orbitals.shape)


def solution(mesh):
    return jax.shard_map(
        local,
        mesh=mesh,
        in_specs=(P(None, "blk", "grp", None), P(), P(), P()),
        out_specs=P(None, "blk", "grp", None),
        check_vma=False,
    )
```

time: 400 us -> 251 us (0.63)
  the two profiles are of different devices: /device:TPU:51 before, /device:TPU:9 now
where the time goes in v2:
time: 251 us; the launch traced here: 250 us
  Pallas kernels  248 us (99%)
  other arithmetic  2.76 us (1%)
    pallas_call x1, Pallas kernels, local(): pl.pallas_call(functools.partial(exchange_kernel, (blocks, size_x, size_y...  243 us

profile of v2, /device:TPU:9, one launch (start us, length us, event | category | flops | bytes accessed | tf_op | source)
XLA Modules:
  0.0 250.4 jit_solution(9685599295435250853)
XLA Ops:
  0.0 1.4 fusion.rows_ref
  1.4 1.4 fusion.1.weight_ref
  2.8 242.9 %shard_map.91.field_ref = f32[64,128,128]{2,1,0:T(8,128)} custom-call(s32[64]{0:T(128)} %fusion.rows_ref, f32[64]{0:T(128)} %fusion.1.weight_ref, f32[64,128,128]{2,1,0:T(8,128)} %bitcast.2, bf16[768,256]{1,0:T(8,128)(2,1)} %constant.14.clone.forward_z_ref, bf16[768,256]{1,0:T(8,128)(2,1)} %constant.15.clone.inverse_z_ref, ...), custom_call_target="tpu_custom_call" | custom-call | tf_op jit(solution)/shard_map/pallas_call | solution.py:399
  245.7 4.7 %shard_map.92 = f32[64,128,128]{2,1,0:T(8,128)} custom-call(s32[64]{0:T(128)} %fusion.rows_ref, f32[64,128,128]{2,1,0:T(8,128)} %shard_map.91.field_ref), custom_call_target="tpu_custom_call" | custom-call | tf_op jit(solution)/shard_map/pallas_call | solution.py:419

commit v3 on v2

--- a/solution.py
+++ b/solution.py
@@ -121,12 +121,14 @@
     sizes,
     rows_ref,
     weight_ref,
-    phi_ref,
+    orbitals_ref,
     forward_z_ref,
     inverse_z_ref,
     left_y_ref,
     forward_x_ref,
     inverse_x_ref,
+    out_ref,
+    phi_ref,
     field_ref,
     outgoing,
     grid,
@@ -137,6 +139,7 @@
     in_sem,
     back_out_sem,
     back_in_sem,
+    load_sem,
 ):
     blocks, size_x, size_y, size_z = sizes
     half_y = size_y // 2
@@ -182,6 +185,8 @@
         for j, target in enumerate(targets(count // 4 - 1)[:3]):
             act(count - 4 + j, target)
 
+    load = pltpu.make_async_copy(orbitals_ref, phi_ref, load_sem)
+    load.start()
     barrier = pltpu.get_barrier_semaphore()
 
     def greet(slot, target):
@@ -189,6 +194,7 @@
 
     every_other(greet)
     pl.semaphore_wait(barrier, count - 1)
+    load.wait()
 
     def density(position, offset):
         first = phi_ref[rows_ref[position]]
@@ -301,6 +307,14 @@
             device_id_type=MESH,
         ).start()
 
+    def turn_all(part):
+        fill_table(part)
+        turn(part, 0, True)
+
+        @pl.loop(1, blocks // 4)
+        def _(index):
+            turn(part, index, False)
+
     def give_back(part, index, sent):
         at = targets(index)
         for target in at:
@@ -308,22 +322,24 @@
         for target in at[:sent]:
             send_back(part, None, target)
 
+    turn_all(0)
+    middle(0)
+
+    @pl.loop(0, count // 4)
+    def _(index):
+        for target in targets(index):
+            turn_back(0, None, target)
+
+    turn_all(1)
+    every_other(functools.partial(send_back, 0))
+    middle(1)
+
+    @pl.loop(0, count // 4 - 1)
+    def _(index):
+        give_back(1, index, 4)
+
+    give_back(1, count // 4 - 1, 3)
     for part in range(2):
-        fill_table(part)
-        turn(part, 0, True)
-
-        @pl.loop(1, blocks // 4)
-        def _(index):
-            turn(part, index, False)
-
-    for part in range(2):
-        middle(part)
-
-        @pl.loop(0, count // 4 - 1)
-        def _(index):
-            give_back(part, index, 4)
-
-        give_back(part, count // 4 - 1, 3)
         arrived[part, me] = grid[part, blk, own_rows]
 
     def collect(index, with_own):
@@ -339,13 +355,13 @@
         value = [jnp.concatenate([arrived[0, k], arrived[1, k]], axis=1) for k in slots]
         value = times_right(jnp.concatenate(value, axis=0), inverse_z_ref[...])
         for j, position in enumerate(at):
-            own = weight_ref[position] * phi_ref[rows_ref[position]]
+            own = weight_ref[rows_ref[position]] * phi_ref[rows_ref[position]]
             total = jnp.zeros((size_y, size_z), f32)
             for side in range(2):
                 behind = (position + blocks - side - 1) % blocks
                 term = value[(2 * j + side) * half_y : (2 * j + side + 1) * half_y]
                 term = jnp.concatenate([term[:, :size_z], term[:, size_z:]], axis=0)
-                total = total + term * (weight_ref[behind] * phi_ref[rows_ref[behind]])
+                total = total + term * (weight_ref[rows_ref[behind]] * phi_ref[rows_ref[behind]])
                 field_ref[behind] += term * own
             field_ref[position] += total
 
@@ -354,22 +370,15 @@
     @pl.loop(1, blocks // 4)
     def _(index):
         collect(index, False)
+
+    @pl.loop(0, blocks)
+    def _(band):
+        out_ref[band] = field_ref[rows_ref[blocks + band]]
 
     for part in range(2):
         sent = outgoing.at[part, pl.ds(0, count - 1)]
         await_copy(sent, out_sem)
         await_copy(sent, back_out_sem)
-
-
-def place_kernel(nbands, rows_ref, field_ref, out_ref, sem):
-    copies = [
-        pltpu.make_async_copy(field_ref.at[p], out_ref.at[rows_ref[p]], sem.at[p])
-        for p in range(nbands)
-    ]
-    for copy in copies:
-        copy.start()
-    for copy in copies:
-        copy.wait()
 
 
 def local(orbitals, occupations, band_block, cycle):
@@ -379,9 +388,12 @@
     size_y = half_y * 2
     plane_rows = local_x * half_y
 
-    here = cycle[:, None] == band_block[None, :]
-    rows = jnp.sum(jnp.where(here, jnp.arange(nbands, dtype=jnp.int32)[None], 0), axis=1)
-    weights = jnp.sum(jnp.where(here, occupations[None], 0.0), axis=1)
+    names = jnp.concatenate([cycle, band_block])
+    listed = jnp.concatenate(
+        [jnp.broadcast_to(v[None], (nbands, nbands)) for v in (band_block, cycle)]
+    )
+    index = jnp.arange(nbands, dtype=jnp.int32)[None]
+    rows = jnp.sum(jnp.where(names[:, None] == listed, index, 0), axis=1)
 
     by_parity = hartley(size_x).reshape(size_x, blocks, 2)
     even_odd = by_parity.transpose(2, 0, 1).reshape(2 * size_x, blocks)
@@ -398,10 +410,12 @@
     smem = pl.BlockSpec(memory_space=pltpu.SMEM)
     field = pl.pallas_call(
         functools.partial(exchange_kernel, (blocks, size_x, size_y, size_z)),
-        out_shape=jax.ShapeDtypeStruct((nbands, plane_rows, size_z), f32),
-        in_specs=[smem, smem] + [vmem] * (1 + len(tables)),
+        out_shape=pltpu.VMEM((nbands, plane_rows, size_z), f32),
+        in_specs=[smem, smem, pl.BlockSpec(memory_space=pl.ANY)] + [vmem] * len(tables),
         out_specs=vmem,
         scratch_shapes=[
+            pltpu.VMEM((nbands, plane_rows, size_z), f32),
+            pltpu.VMEM((nbands, plane_rows, size_z), f32),
             pltpu.VMEM((2, 2 * blocks, half_y, size_z), f32),
             pltpu.VMEM((2, blocks, size_y, size_z), f32),
             pltpu.VMEM((2, size_y * blocks, size_z), f32),
@@ -411,19 +425,13 @@
             pltpu.SemaphoreType.DMA((2, blocks)),
             pltpu.SemaphoreType.DMA,
             pltpu.SemaphoreType.DMA((2, blocks)),
+            pltpu.SemaphoreType.DMA,
         ],
         compiler_params=pltpu.CompilerParams(
-            collective_id=0, has_side_effects=True, vmem_limit_bytes=60 * MIB
+            collective_id=0, has_side_effects=True, vmem_limit_bytes=55 * MIB
         ),
-    )(rows, weights, orbitals.reshape(nbands, plane_rows, size_z), *tables)
-    placed = pl.pallas_call(
-        functools.partial(place_kernel, nbands),
-        out_shape=jax.ShapeDtypeStruct((nbands, plane_rows, size_z), f32),
-        in_specs=[smem, vmem],
-        out_specs=pl.BlockSpec(memory_space=pl.ANY),
-        scratch_shapes=[pltpu.SemaphoreType.DMA((nbands,))],
-    )(rows, field)
-    return placed.reshape(orbitals.shape)
+    )(rows, occupations, orbitals.reshape(nbands, plane_rows, size_z), *tables)
+    return field.reshape(orbitals.shape)
 
 
 def solution(mesh):

time: 251 us -> 235 us (0.936)
  the two profiles are of different devices: /device:TPU:9 before, /device:TPU:15 now
where the time goes in v3:
time: 235 us; the launch traced here: 234 us
  Pallas kernels  229 us (97%)
  local copies, waits for them, and re-layouts  3.47 us (1%)
    pallas_call x1, Pallas kernels, local(): pl.pallas_call(functools.partial(exchange_kernel, (blocks, size_x, size_y...  229 us

profile of v3, /device:TPU:15, one launch (start us, length us, event | category | flops | bytes accessed | tf_op | source)
XLA Modules:
  0.0 233.9 jit_solution(5197512926084267849)
XLA Ops:
  0.0 0.7 pad_add_fusion
  0.7 0.7 broadcast_in_dim.12
  1.5 0.7 broadcast_in_dim.13
  2.2 0.6 select_reduce_fusion.rows_ref
  2.8 229.0 %shard_map.91 = f32[64,128,128]{2,1,0:T(8,128)S(1)} custom-call(s32[128]{0:T(128)} %select_reduce_fusion.rows_ref, f32[64]{0:T(128)} %weight_ref.1, f32[64,128,128]{2,1,0:T(8,128)} %bitcast.3, bf16[768,256]{1,0:T(8,128)(2,1)} %constant.12.clone.forward_z_ref, bf16[768,256]{1,0:T(8,128)(2,1)} %constant.13.clone.inverse_z_ref, ...), custom_call_target="tpu_custom_call" | custom-call | tf_op jit(solution)/shard_map/pallas_call | solution.py:411
  231.8 2.0 copy.11

commit v4 on v3

--- a/solution.py
+++ b/solution.py
@@ -119,8 +119,9 @@
 
 def exchange_kernel(
     sizes,
-    rows_ref,
     weight_ref,
+    band_block_ref,
+    cycle_ref,
     orbitals_ref,
     forward_z_ref,
     inverse_z_ref,
@@ -140,6 +141,9 @@
     back_out_sem,
     back_in_sem,
     load_sem,
+    listing,
+    listed,
+    list_sem,
 ):
     blocks, size_x, size_y, size_z = sizes
     half_y = size_y // 2
@@ -187,6 +191,17 @@
 
     load = pltpu.make_async_copy(orbitals_ref, phi_ref, load_sem)
     load.start()
+
+    listing[...] = jnp.zeros_like(listing)
+    for row, (named, among) in enumerate(((cycle_ref, band_block_ref), (band_block_ref, cycle_ref))):
+        named = jnp.broadcast_to(named[...], (blocks, blocks))
+        among = jnp.broadcast_to(among[...], (blocks, blocks)).T
+        index = lax.broadcasted_iota(jnp.int32, (blocks, blocks), 0)
+        found = jnp.max(jnp.where(named == among, index, 0), axis=0, keepdims=True)
+        listing[row : row + 1, :blocks] = found
+    to_scalars = pltpu.make_async_copy(listing, listed, list_sem)
+    to_scalars.start()
+
     barrier = pltpu.get_barrier_semaphore()
 
     def greet(slot, target):
@@ -195,10 +210,11 @@
     every_other(greet)
     pl.semaphore_wait(barrier, count - 1)
     load.wait()
+    to_scalars.wait()
 
     def density(position, offset):
-        first = phi_ref[rows_ref[position]]
-        second = phi_ref[rows_ref[(position + blocks - offset) % blocks]]
+        first = phi_ref[listed[0, position]]
+        second = phi_ref[listed[0, (position + blocks - offset) % blocks]]
         value = first * second
         return jnp.concatenate([value[:half_y], value[half_y:]], axis=1)
 
@@ -253,13 +269,15 @@
     def await_copy(ref, sem):
         pltpu.make_async_copy(ref, ref, sem).wait()
 
-    def turn(part, index, with_own):
+    def turn(part, index, with_own, between=None):
         at = source_blocks(index)
         for j, source in enumerate(at):
             if with_own and j == 0:
                 await_copy(grid.at[part, blk, own_rows], in_sem.at[part, blk])
             else:
                 await_copy(grid.at[part, source], in_sem.at[part, source])
+        if between is not None:
+            between()
         value = jnp.concatenate([grid[part, source] for source in at], axis=1)
         value = times_left(left_y_ref[...], value)
         for j, source in enumerate(at):
@@ -307,13 +325,15 @@
             device_id_type=MESH,
         ).start()
 
-    def turn_all(part):
+    def turn_all(part, then=None):
         fill_table(part)
         turn(part, 0, True)
 
-        @pl.loop(1, blocks // 4)
+        @pl.loop(1, blocks // 4 - 1)
         def _(index):
             turn(part, index, False)
+
+        turn(part, blocks // 4 - 1, False, then)
 
     def give_back(part, index, sent):
         at = targets(index)
@@ -330,8 +350,10 @@
         for target in targets(index):
             turn_back(0, None, target)
 
-    turn_all(1)
-    every_other(functools.partial(send_back, 0))
+    def start_return():
+        every_other(functools.partial(send_back, 0))
+
+    turn_all(1, start_return)
     middle(1)
 
     @pl.loop(0, count // 4 - 1)
@@ -355,13 +377,13 @@
         value = [jnp.concatenate([arrived[0, k], arrived[1, k]], axis=1) for k in slots]
         value = times_right(jnp.concatenate(value, axis=0), inverse_z_ref[...])
         for j, position in enumerate(at):
-            own = weight_ref[rows_ref[position]] * phi_ref[rows_ref[position]]
+            own = weight_ref[listed[0, position]] * phi_ref[listed[0, position]]
             total = jnp.zeros((size_y, size_z), f32)
             for side in range(2):
                 behind = (position + blocks - side - 1) % blocks
                 term = value[(2 * j + side) * half_y : (2 * j + side + 1) * half_y]
                 term = jnp.concatenate([term[:, :size_z], term[:, size_z:]], axis=0)
-                total = total + term * (weight_ref[rows_ref[behind]] * phi_ref[rows_ref[behind]])
+                total = total + term * (weight_ref[listed[0, behind]] * phi_ref[listed[0, behind]])
                 field_ref[behind] += term * own
             field_ref[position] += total
 
@@ -373,7 +395,7 @@
 
     @pl.loop(0, blocks)
     def _(band):
-        out_ref[band] = field_ref[rows_ref[blocks + band]]
+        out_ref[band] = field_ref[listed[1, band]]
 
     for part in range(2):
         sent = outgoing.at[part, pl.ds(0, count - 1)]
@@ -387,13 +409,6 @@
     size_x = local_x * blocks
     size_y = half_y * 2
     plane_rows = local_x * half_y
-
-    names = jnp.concatenate([cycle, band_block])
-    listed = jnp.concatenate(
-        [jnp.broadcast_to(v[None], (nbands, nbands)) for v in (band_block, cycle)]
-    )
-    index = jnp.arange(nbands, dtype=jnp.int32)[None]
-    rows = jnp.sum(jnp.where(names[:, None] == listed, index, 0), axis=1)
 
     by_parity = hartley(size_x).reshape(size_x, blocks, 2)
     even_odd = by_parity.transpose(2, 0, 1).reshape(2 * size_x, blocks)
@@ -411,7 +426,7 @@
     field = pl.pallas_call(
         functools.partial(exchange_kernel, (blocks, size_x, size_y, size_z)),
         out_shape=pltpu.VMEM((nbands, plane_rows, size_z), f32),
-        in_specs=[smem, smem, pl.BlockSpec(memory_space=pl.ANY)] + [vmem] * len(tables),
+        in_specs=[smem, vmem, vmem, pl.BlockSpec(memory_space=pl.ANY)] + [vmem] * len(tables),
         out_specs=vmem,
         scratch_shapes=[
             pltpu.VMEM((nbands, plane_rows, size_z), f32),
@@ -426,11 +441,20 @@
             pltpu.SemaphoreType.DMA,
             pltpu.SemaphoreType.DMA((2, blocks)),
             pltpu.SemaphoreType.DMA,
+            pltpu.VMEM((8, 128), jnp.int32),
+            pltpu.SMEM((8, 128), jnp.int32),
+            pltpu.SemaphoreType.DMA,
         ],
         compiler_params=pltpu.CompilerParams(
             collective_id=0, has_side_effects=True, vmem_limit_bytes=55 * MIB
         ),
-    )(rows, occupations, orbitals.reshape(nbands, plane_rows, size_z), *tables)
+    )(
+        occupations,
+        band_block.reshape(1, nbands),
+        cycle.reshape(1, nbands),
+        orbitals.reshape(nbands, plane_rows, size_z),
+        *tables,
+    )
     return field.reshape(orbitals.shape)
 
 

time: 235 us -> 232 us (0.987)
  no operation moved by 1% of the time
where the time goes in v4:
time: 232 us; the launch traced here: 230 us
  Pallas kernels  228 us (98%)
    pallas_call x1, Pallas kernels, local(): pl.pallas_call(functools.partial(exchange_kernel, (blocks, size_x, size_y...  228 us

profile of v4, /device:TPU:15, one launch (start us, length us, event | category | flops | bytes accessed | tf_op | source)
XLA Modules:
  0.0 230.5 jit_solution(16259652696049294619)
XLA Ops:
  0.0 228.5 %shard_map.91 = f32[64,128,128]{2,1,0:T(8,128)S(1)} custom-call(f32[64]{0:T(128)} %weight_ref.1, s32[1,64]{1,0:T(1,128)} %bitcast.6, s32[1,64]{1,0:T(1,128)} %bitcast.7, f32[64,128,128]{2,1,0:T(8,128)} %bitcast.5, bf16[768,256]{1,0:T(8,128)(2,1)} %constant.10.clone.forward_z_ref, bf16[768,256]{1,0:T(8,128)(2,1)} %constant.11.clone.inverse_z_ref, ...), custom_call_target="tpu_custom_call" | custom-call | tf_op jit(solution)/shard_map/pallas_call | solution.py:426
  228.5 2.0 copy.11
